TPU v7x, 256 devices: a whole 4x4x8 slice. The times are simulated.
256 devices in a mesh: dp: 32 (over z_lo, x, core), rows: 8 (over z_hi, y).
Axes of the slice: x: 4, y: 4, z: 8 (z_hi: 2, z_lo: 4; z = z_hi * 4 + z_lo), core: 2. Of those that a mesh axis runs over, the one named last changes fastest.
Arguments:
- features: bfloat16 [64, 48, 64, 1024], P('dp', 'rows'), may hold values from -8 to 8
- first_atrous_weight: bfloat16 [3, 3, 1024, 256], P(None, None, 'dp'), may hold values from -0.0625 to 0.0625
- second_atrous_weight: bfloat16 [3, 3, 1024, 256], P(None, None, 'dp'), may hold values from -0.0625 to 0.0625
- third_atrous_weight: bfloat16 [3, 3, 1024, 256], P(None, None, 'dp'), may hold values from -0.0625 to 0.0625
- pointwise_weight: bfloat16 [1024, 256], replicated, may hold values from -0.1875 to 0.1875
- pooling_weight: bfloat16 [1024, 256], replicated, may hold values from -0.1875 to 0.1875
- projection_weight: bfloat16 [1280, 256], replicated, may hold values from -0.15625 to 0.15625
- branch_norm_gain: float32 [4, 256], replicated, may hold values from 0.25 to 1.75
- branch_norm_shift: float32 [4, 256], replicated, may hold values from -3 to 3
- projection_norm_gain: float32 [256], replicated, may hold values from 0.25 to 1.75
- projection_norm_shift: float32 [256], replicated, may hold values from -3 to 3
- ghost_group_index: int32 [64], replicated, may hold values from 0 to 15, as said below
Outputs:
- decoder_in: bfloat16 [64, 48, 64, 256], P(None, 'rows', 'dp')
Inputs may be any that keep to these rules, and one draw needn't show every extreme that they name: `ghost_group_index`: each of the 16 group ids names exactly 4 images.
All inputs are finite; a program needn't handle non-finite values.
Results may differ from a plain program's by a relative error of at most 0.0014.
The roundings to bfloat16 on the way count: a program that leaves them out, or rounds other values in their place, can miss the bound.
Values may be sent and summed in bfloat16 or wider, within the bound.
A program may use at most 128 MiB of HBM per device.

v0:
```python
import jax
import jax.numpy as jnp
from jax import lax
from jax.sharding import PartitionSpec as P

DILATION_FIRST = 12
DILATION_SECOND = 24
DILATION_THIRD = 36


def from_behind(array, axis, by):
    count = lax.axis_size(axis)
    pairs = [(i, i + by) for i in range(count) if 0 <= i + by < count]
    return lax.ppermute(array, axis, pairs)


def row_tap_list(block_tensor, kernel_row_slice, dilation_rate):
    partial_terms = jnp.einsum(
        "irwc,kco->irwko", block_tensor, kernel_row_slice, preferred_element_type=jnp.float32
    )
    map_width = block_tensor.shape[2]
    left_padding = jnp.pad(partial_terms[:, :, :, 0], ((0, 0), (0, 0), (dilation_rate, 0), (0, 0)))[
        :, :, :map_width
    ]
    right_padding = jnp.pad(
        partial_terms[:, :, :, 2], ((0, 0), (0, 0), (0, dilation_rate), (0, 0))
    )[:, :, dilation_rate:]
    return partial_terms[:, :, :, 1] + left_padding + right_padding


def dilated_result(features, kernel_weight, dilation_rate):
    step_offsets = dilation_rate // features.shape[1]
    running_sum = row_tap_list(features, kernel_weight[1], dilation_rate)
    for by_dev, tap_offset in ((step_offsets, 0), (-step_offsets, 2)):
        shifted_rows = from_behind(features, "rows", by_dev)
        running_sum = running_sum + row_tap_list(
            shifted_rows, kernel_weight[tap_offset], dilation_rate
        )
    return running_sum


def stats_terms(pre, onehot):
    first = jnp.sum(pre, axis=(1, 2))
    second = jnp.sum(pre * pre, axis=(1, 2))
    group_first = jnp.dot(onehot.T, first, precision=lax.Precision.HIGHEST)
    group_second = jnp.dot(onehot.T, second, precision=lax.Precision.HIGHEST)
    return (group_first, group_second)


def apply_norm(pre, onehot, total_first, total_second, count, gain, shift):
    mean = total_first / count
    var = total_second / count - mean * mean
    inv = lax.rsqrt(var + 1e-05)
    img_mean = jnp.dot(onehot, mean, precision=lax.Precision.HIGHEST)
    img_inv = jnp.dot(onehot, inv, precision=lax.Precision.HIGHEST)
    scaled = (pre - img_mean[:, None, None, :]) * img_inv[:, None, None, :] * gain + shift
    return jax.nn.relu(scaled).astype(jnp.bfloat16)


def project(joined, onehot, projection_weight, count, projection_norm_gain, projection_norm_shift):
    proj = jnp.einsum(
        "irwc,co->irwo", joined, projection_weight, preferred_element_type=jnp.float32
    )
    group_first, group_second = stats_terms(proj, onehot)
    total_first, total_second = lax.psum((group_first, group_second), ("dp", "rows"))
    return apply_norm(
        proj, onehot, total_first, total_second, count, projection_norm_gain, projection_norm_shift
    )


def shards(
    features,
    first_atrous_weight,
    second_atrous_weight,
    third_atrous_weight,
    pointwise_weight,
    pooling_weight,
    projection_weight,
    branch_norm_gain,
    branch_norm_shift,
    projection_norm_gain,
    projection_norm_shift,
    ghost_group_index,
):
    img_dev, rows_dev, cols, chans = features.shape
    dp_size = lax.axis_size("dp")
    rows_size = lax.axis_size("rows")
    images = img_dev * dp_size
    groups = images // 4
    pixels = rows_dev * rows_size * cols
    count = 4.0 * pixels
    start = lax.axis_index("dp") * img_dev
    labels = jnp.arange(groups, dtype=jnp.int32)
    all_hot = (ghost_group_index[:, None] == labels[None, :]).astype(jnp.float32)
    own_hot = lax.dynamic_slice_in_dim(all_hot, start, img_dev, 0)
    first_kernel, second_kernel, third_kernel = (
        lax.all_gather(first_atrous_weight, "dp", axis=2, tiled=True),
        lax.all_gather(second_atrous_weight, "dp", axis=2, tiled=True),
        lax.all_gather(third_atrous_weight, "dp", axis=2, tiled=True),
    )
    pointwise_output = jnp.einsum(
        "irwc,co->irwo", features, pointwise_weight, preferred_element_type=jnp.float32
    )
    pre = jnp.concatenate(
        [
            pointwise_output,
            dilated_result(features, first_kernel, DILATION_FIRST),
            dilated_result(features, second_kernel, DILATION_SECOND),
            dilated_result(features, third_kernel, DILATION_THIRD),
        ],
        -1,
    )
    group_first, group_second = stats_terms(pre, own_hot)
    pool_part = jnp.sum(features, axis=(1, 2), dtype=jnp.float32)
    pool_total = lax.psum(pool_part, "rows")
    total_first, total_second = lax.psum((group_first, group_second), ("dp", "rows"))
    branches = apply_norm(
        pre,
        own_hot,
        total_first,
        total_second,
        count,
        branch_norm_gain.reshape(-1),
        branch_norm_shift.reshape(-1),
    )
    pooled = (pool_total / pixels).astype(jnp.bfloat16)
    pool_act = jax.nn.relu(
        jnp.dot(pooled, pooling_weight, preferred_element_type=jnp.float32)
    ).astype(jnp.bfloat16)
    pool_map = jnp.broadcast_to(
        pool_act[:, None, None, :], (img_dev, rows_dev, cols, pool_act.shape[1])
    )
    joined = jnp.concatenate([branches, pool_map], -1)
    local_out = project(
        joined, own_hot, projection_weight, count, projection_norm_gain, projection_norm_shift
    )
    return lax.all_to_all(local_out, "dp", split_axis=2, concat_axis=0, tiled=True)


def solution(mesh):
    in_specs = (
        P("dp", "rows", None, None),
        P(None, None, "dp", None),
        P(None, None, "dp", None),
        P(None, None, "dp", None),
        P(),
        P(),
        P(),
        P(),
        P(),
        P(),
        P(),
        P(),
    )
    out_specs = P(None, "rows", "dp", None)
    return jax.shard_map(shards, mesh=mesh, in_specs=in_specs, out_specs=out_specs, check_vma=False)
```

profile of v0, /device:TPU:1, one launch (start us, length us, event | category | flops | bytes accessed | tf_op | source)
XLA Modules:
  0.0 726.8 jit_solution(7017526560821502395)
XLA Ops:
  8.8 1.3 collective-permute-start.1
  10.1 7.5 %collective-permute-start = (bf16[2,6,64,1024]{3,2,1,0:T(8,128)(2,1)}, bf16[2,6,64,1024]{3,2,1,0:T(8,128)(2,1)}, u32[]{:S(2)}, u32[]{:S(2)}) collective-permute-start(bf16[2,6,64,1024]{3,2,1,0:T(8,128)(2,1)} %param.12), channel_id=1, source_target_pairs={{0,2},{1,3},{2,4},{3,5},{4,6},{5,7},{8,10},{9,11},{10,12},{11,13},... | collective-permute-start | bytes 4718600 | tf_op jit(solution)/shard_map/ppermute | solution.py:14
  17.6 1.3 collective-permute-start.3
  18.9 11.2 %collective-permute-start.2 = (bf16[2,6,64,1024]{3,2,1,0:T(8,128)(2,1)}, bf16[2,6,64,1024]{3,2,1,0:T(8,128)(2,1)}, u32[]{:S(2)}, u32[]{:S(2)}) collective-permute-start(bf16[2,6,64,1024]{3,2,1,0:T(8,128)(2,1)} %param.12), channel_id=1, source_target_pairs={{0,4},{1,5},{2,6},{3,7},{8,12},{9,13},{10,14},{11,15},{16,20},{17,... | collective-permute-start | bytes 4718600 | tf_op jit(solution)/shard_map/ppermute | solution.py:14
  30.1 1.3 collective-permute-start.5
  32.1 1.7 convert_reduce_fusion
  33.9 146.7 %psum.37 = f32[2,1024]{1,0:T(2,128)S(1)} all-reduce(f32[2,1024]{1,0:T(2,128)S(1)} %convert_reduce_fusion), channel_id=1, replica_groups=mesh['dp'=32,'rows'=8] {'rows'}, use_global_device_ids=true, to_apply=%region_5.6 | all-reduce | flops 2048 | bytes 16384 | tf_op jit(solution)/shard_map/psum | solution.py:115
  180.5 2.1 fusion.49
  182.7 2.4 collective-permute-start.4
  185.1 3.4 fusion.10
  188.5 1.4 slice_bitcast_fusion.36
  189.9 2.8 fusion.11
  192.7 1.4 slice_bitcast_fusion.39
  194.1 1.4 fusion.12
  195.5 1.3 slice_bitcast_fusion.42
  197.4 90.0 %all-gather.6.cloned.1.call-done = bf16[3,3,1024,256]{3,2,1,0:T(8,128)(2,1)} async-done(((bf16[3,3,32,256]{3,2,1,0:T(8,128)(2,1)}), bf16[3,3,1024,256]{3,2,1,0:T(8,128)(2,1)}) %all-gather.6.cloned.1.call-update) | async-done | bytes 4718608 | tf_op jit(solution)/shard_map/all_gather | solution.py:98
  287.4 3.4 fusion.7
  290.8 1.4 slice_bitcast_fusion.27
  292.3 2.8 fusion.8
  295.1 1.4 slice_bitcast_fusion.30
  296.5 1.4 fusion.9
  297.9 1.5 slice_bitcast_fusion.33
  299.8 61.1 %all-gather.8.cloned.1.call-done = bf16[3,3,1024,256]{3,2,1,0:T(8,128)(2,1)} async-done(((bf16[3,3,32,256]{3,2,1,0:T(8,128)(2,1)}), bf16[3,3,1024,256]{3,2,1,0:T(8,128)(2,1)}) %all-gather.8.cloned.1.call-update) | async-done | bytes 4718608 | tf_op jit(solution)/shard_map/all_gather | solution.py:99
  361.0 3.4 fusion.4
  364.5 2.8 fusion.5
  367.5 1.4 fusion.6
  370.8 2.3 fusion.26
  373.8 1.9 fusion.34
  381.0 237.9 %all-reduce.22.cloned.1.call-done = (f32[16,1024]{1,0:T(8,128)}, f32[16,1024]{1,0:T(8,128)}) async-done(((f32[16,1024]{1,0:T(8,128)}, f32[16,1024]{1,0:T(8,128)}), (f32[16,1024]{1,0:T(8,128)}, f32[16,1024]{1,0:T(8,128)})) %all-reduce.22.cloned.1.call-update) | async-done | bytes 131088 | tf_op jit(solution)/shard_map/psum | solution.py:116
  621.0 1.7 maximum_convert_fusion
  624.1 76.6 %all-reduce.18 = (f32[16,256]{1,0:T(8,128)S(1)}, f32[16,256]{1,0:T(8,128)S(1)}) all-reduce(f32[16,256]{1,0:T(8,128)S(1)} %fusion.76, f32[16,256]{1,0:T(8,128)S(1)} %fusion.77), channel_id=1, replica_groups=mesh['dp'=32,'rows'=8] {'dp','rows'}, use_global_device_ids=true, to_apply=%region_9.10 | all-reduce | flops 8192 | bytes 65536 | tf_op jit(solution)/shard_map/psum | solution.py:65
  701.6 17.6 %all_to_all.18 = bf16[2,6,64,256]{3,0,1,2:T(2,128)(2,1)S(1)} all-to-all(bf16[2,6,64,256]{3,0,1,2:T(2,128)(2,1)S(1)} %copy.97), channel_id=1, replica_groups=mesh['dp'=32,'rows'=8] {'dp'}, dimensions={2} | all-to-all | bytes 786432 | tf_op jit(solution)/shard_map/all_to_all | solution.py:137
  (91 shorter events, 17.6 us)
Async XLA Ops:
  6.5 616.3 %copy-start = (bf16[1280,256]{1,0:T(8,128)(2,1)S(1)}, bf16[1280,256]{1,0:T(8,128)(2,1)}, u32[]{:S(2)}) copy-start(bf16[1280,256]{1,0:T(8,128)(2,1)} %param.18) | copy-start | bytes 1966084
  6.5 178.6 %all-gather.4.cloned.1.call-start = ((), (), s32[]{:S(2)}) async-start(), calls=%async_computation.1 | async-start | bytes 4866048 | tf_op jit(solution)/shard_map/all_gather | solution.py:97
  7.3 280.2 %all-gather.6.cloned.1.call-start = ((), (), s32[]{:S(2)}) async-start(), calls=%async_computation.2 | async-start | bytes 4866048 | tf_op jit(solution)/shard_map/all_gather | solution.py:98
  8.0 174.6 %copy-start.2 = (bf16[2,6,64,1024]{3,2,1,0:T(8,128)(2,1)S(1)}, bf16[2,6,64,1024]{3,2,1,0:T(8,128)(2,1)}, u32[]{:S(2)}) copy-start(bf16[2,6,64,1024]{3,2,1,0:T(8,128)(2,1)} %param.12) | copy-start | bytes 4718596
  8.0 352.9 %all-gather.8.cloned.1.call-start = ((), (), s32[]{:S(2)}) async-start(), calls=%async_computation.3 | async-start | bytes 4866048 | tf_op jit(solution)/shard_map/all_gather | solution.py:99
  8.8 610.2 %all-reduce.22.cloned.1.call-start = ((), (), s32[]{:S(2)}) async-start(), calls=%async_computation.4 | async-start | bytes 262144 | tf_op jit(solution)/shard_map/psum | solution.py:116
  8.8 173.8 %collective-permute-start.1 = (bf16[2,6,64,1024]{3,2,1,0:T(8,128)(2,1)}, bf16[2,6,64,1024]{3,2,1,0:T(8,128)(2,1)}, u32[]{:S(2)}, u32[]{:S(2)}) collective-permute-start(bf16[2,6,64,1024]{3,2,1,0:T(8,128)(2,1)} %param.12), channel_id=1, source_target_pairs={{2,0},{3,1},{4,2},{5,3},{6,4},{7,5},{10,8},{11,9},{12,10},{13,11},... | collective-permute-start | bytes 4718600 | tf_op jit(solution)/shard_map/ppermute | solution.py:14
  10.1 179.8 %collective-permute-start = (bf16[2,6,64,1024]{3,2,1,0:T(8,128)(2,1)}, bf16[2,6,64,1024]{3,2,1,0:T(8,128)(2,1)}, u32[]{:S(2)}, u32[]{:S(2)}) collective-permute-start(bf16[2,6,64,1024]{3,2,1,0:T(8,128)(2,1)} %param.12), channel_id=1, source_target_pairs={{0,2},{1,3},{2,4},{3,5},{4,6},{5,7},{8,10},{9,11},{10,12},{11,13},... | collective-permute-start | bytes 4718600 | tf_op jit(solution)/shard_map/ppermute | solution.py:14
  17.6 179.9 %collective-permute-start.3 = (bf16[2,6,64,1024]{3,2,1,0:T(8,128)(2,1)}, bf16[2,6,64,1024]{3,2,1,0:T(8,128)(2,1)}, u32[]{:S(2)}, u32[]{:S(2)}) collective-permute-start(bf16[2,6,64,1024]{3,2,1,0:T(8,128)(2,1)} %param.12), channel_id=1, source_target_pairs={{4,0},{5,1},{6,2},{7,3},{12,8},{13,9},{14,10},{15,11},{20,16},{21,... | collective-permute-start | bytes 4718600 | tf_op jit(solution)/shard_map/ppermute | solution.py:14
  18.9 273.4 %collective-permute-start.2 = (bf16[2,6,64,1024]{3,2,1,0:T(8,128)(2,1)}, bf16[2,6,64,1024]{3,2,1,0:T(8,128)(2,1)}, u32[]{:S(2)}, u32[]{:S(2)}) collective-permute-start(bf16[2,6,64,1024]{3,2,1,0:T(8,128)(2,1)} %param.12), channel_id=1, source_target_pairs={{0,4},{1,5},{2,6},{3,7},{8,12},{9,13},{10,14},{11,15},{16,20},{17,... | collective-permute-start | bytes 4718600 | tf_op jit(solution)/shard_map/ppermute | solution.py:14
  30.1 269.7 %collective-permute-start.5 = (bf16[2,6,64,1024]{3,2,1,0:T(8,128)(2,1)}, bf16[2,6,64,1024]{3,2,1,0:T(8,128)(2,1)}, u32[]{:S(2)}, u32[]{:S(2)}) collective-permute-start(bf16[2,6,64,1024]{3,2,1,0:T(8,128)(2,1)} %param.12), channel_id=1, source_target_pairs={{6,0},{7,1},{14,8},{15,9},{22,16},{23,17},{30,24},{31,25},{38,32},... | collective-permute-start | bytes 4718600 | tf_op jit(solution)/shard_map/ppermute | solution.py:14
  182.7 181.9 %collective-permute-start.4 = (bf16[2,6,64,1024]{3,2,1,0:T(8,128)(2,1)S(1)}, bf16[2,6,64,1024]{3,2,1,0:T(8,128)(2,1)}, u32[]{:S(2)}, u32[]{:S(2)}) collective-permute-start(bf16[2,6,64,1024]{3,2,1,0:T(8,128)(2,1)S(1)} %copy-done.2), channel_id=1, source_target_pairs={{0,6},{1,7},{8,14},{9,15},{16,22},{17,23},{24,30},{25,31},{32,38},... | collective-permute-start | bytes 4718600 | tf_op jit(solution)/shard_map/ppermute | solution.py:14
  185.1 4.8 copy-start.26
  188.5 4.2 copy-start.15
  192.7 2.8 copy-start.16
  195.5 2.0 copy-start.17
  287.4 4.8 copy-start.25
  290.8 4.2 copy-start.18
  295.1 2.8 copy-start.19
  297.9 2.0 copy-start.20
  361.0 3.6 copy-start.24
  367.5 1.6 copy-start.7
  368.9 1.8 copy-start.6
  370.8 2.3 copy-start.9
  370.8 2.3 copy-start.10
  370.8 2.3 copy-start.11
  370.8 2.5 copy-start.12
  370.8 2.8 copy-start.13
  370.8 3.0 copy-start.14
  377.2 2.2 copy-start.21
  622.8 78.2 %copy-start.22 = (f32[256]{0:T(256)S(1)}, f32[256]{0:T(256)}, u32[]{:S(2)}) copy-start(f32[256]{0:T(256)} %param.22) | copy-start | bytes 3076
  622.8 78.2 %copy-start.23 = (f32[256]{0:T(256)S(1)}, f32[256]{0:T(256)}, u32[]{:S(2)}) copy-start(f32[256]{0:T(256)} %param.21) | copy-start | bytes 3076
  (5 other events, 6.6 us)
Sparse Core Ops, SparseCore 0:
  9.2 144.8 all-gather.3
  156.0 131.4 all-gather.5
  289.3 71.6 all-gather.7
  379.6 239.3 all-reduce.21
where the time goes:
time: 728 us; the launch traced here: 727 us
  waiting for transfers between devices  391 us (54%)
  blocking collectives  241 us (33%)
  matrix products  30.6 us (4%)
  starting transfers between devices  25.1 us (3%)
  local copies, waits for them, and re-layouts  16.8 us (2%)
  between operations  13.6 us (2%)
  other arithmetic  8.76 us (1%)
    psum x1, waiting for transfers between devices, shards(): lax.psum((group_first, group_second), ('dp', 'rows'))  238 us
    psum x1, blocking collectives, shards(): pool_total = lax.psum(pool_part, 'rows')  147 us
    all_gather x1, waiting for transfers between devices, shards(): lax.all_gather(second_atrous_weight, 'dp', axis=2, tiled=True)  90 us
    psum x1, blocking collectives, project(): lax.psum((group_first, group_second), ('dp', 'rows'))  76.6 us
    all_gather x1, waiting for transfers between devices, shards(): lax.all_gather(third_atrous_weight, 'dp', axis=2, tiled=True)  61.1 us
    ppermute x6, starting transfers between devices, from_behind(): return lax.ppermute(array, axis, pairs)  25 us
    dot_general x9, matrix products, row_tap_list(): jnp.einsum('irwc,kco->irwko', block_tensor, kernel_row_slice, preferred_e...  22.8 us
    all_to_all x1, blocking collectives, shards(): lax.all_to_all(local_out, 'dp', split_axis=2, concat_axis=0, tiled=True)  17.6 us
  transfers between devices with their start and end apart: 10, of which 3 were waited for; matrix products, arithmetic and copies ran while one was open for 5% of the time, Pallas kernels for 0%

commit v1 on v0

--- a/solution.py
+++ b/solution.py
@@ -62,7 +62,9 @@
         "irwc,co->irwo", joined, projection_weight, preferred_element_type=jnp.float32
     )
     group_first, group_second = stats_terms(proj, onehot)
-    total_first, total_second = lax.psum((group_first, group_second), ("dp", "rows"))
+    total_first, total_second = jax.lax.psum(
+        jax.lax.psum((group_first, group_second), axis_name="rows"), axis_name="dp"
+    )
     return apply_norm(
         proj, onehot, total_first, total_second, count, projection_norm_gain, projection_norm_shift
     )

time: 728 us -> 836 us (1.15)
  blocking collectives: 241 us -> 349 us
    psum x1 -> x2, blocking collectives: 76.6 us -> 179 us  [the longest x1 135 us: project(): jax.lax.psum(jax.lax.psum((group_first, group_second), axis_name='rows'),...]
  transfers between devices with their start and end apart: 10 -> 10, of which waited for: 3 -> 3; matrix products, arithmetic and copies ran while one was open for 5% -> 4% of each run, Pallas kernels for 0% -> 0%
where the time goes in v1:
time: 836 us
  waiting for transfers between devices  392 us (47%)
  blocking collectives  349 us (42%)
  matrix products  30.6 us (4%)
  starting transfers between devices  25.1 us (3%)
  local copies, waits for them, and re-layouts  16.8 us (2%)
  between operations  13.6 us (2%)
  other arithmetic  8.76 us (1%)
    psum x1, waiting for transfers between devices, shards(): lax.psum((group_first, group_second), ('dp', 'rows'))  238 us
    psum x1, blocking collectives, shards(): pool_total = lax.psum(pool_part, 'rows')  147 us
    psum x1, blocking collectives, project(): jax.lax.psum(jax.lax.psum((group_first, group_second), axis_name='rows'),...  135 us
    all_gather x1, waiting for transfers between devices, shards(): lax.all_gather(second_atrous_weight, 'dp', axis=2, tiled=True)  88.2 us
    all_gather x1, waiting for transfers between devices, shards(): lax.all_gather(third_atrous_weight, 'dp', axis=2, tiled=True)  63.8 us
    psum x1, blocking collectives, project(): jax.lax.psum((group_first, group_second), axis_name='rows')  44.1 us
    ppermute x6, starting transfers between devices, from_behind(): return lax.ppermute(array, axis, pairs)  25 us
    all_to_all x1, blocking collectives, shards(): lax.all_to_all(local_out, 'dp', split_axis=2, concat_axis=0, tiled=True)  22.8 us
  transfers between devices with their start and end apart: 10, of which 3 were waited for; matrix products, arithmetic and copies ran while one was open for 4% of the time, Pallas kernels for 0%

profile of v1, /device:TPU:1, one launch (start us, length us, event | category | flops | bytes accessed | tf_op | source)
XLA Modules:
  0.0 835.5 jit_solution(3345358283914562463)
XLA Ops:
  8.8 1.3 collective-permute-start.1
  10.1 7.5 collective-permute-start
  17.6 1.3 collective-permute-start.3
  18.9 11.3 %collective-permute-start.2 = (bf16[2,6,64,1024]{3,2,1,0:T(8,128)(2,1)}, bf16[2,6,64,1024]{3,2,1,0:T(8,128)(2,1)}, u32[]{:S(2)}, u32[]{:S(2)}) collective-permute-start(bf16[2,6,64,1024]{3,2,1,0:T(8,128)(2,1)} %param.12), channel_id=1, source_target_pairs={{0,4},{1,5},{2,6},{3,7},{8,12},{9,13},{10,14},{11,15},{16,20},{17,... | collective-permute-start | bytes 4718600 | tf_op jit(solution)/shard_map/ppermute | solution.py:14
  32.2 1.7 convert_reduce_fusion
  33.9 146.6 %psum.51 = f32[2,1024]{1,0:T(2,128)S(1)} all-reduce(f32[2,1024]{1,0:T(2,128)S(1)} %convert_reduce_fusion), channel_id=1, replica_groups=mesh['dp'=32,'rows'=8] {'rows'}, use_global_device_ids=true, to_apply=%region_5.6 | all-reduce | flops 2048 | bytes 16384 | tf_op jit(solution)/shard_map/psum | solution.py:117
  180.5 2.1 fusion.49
  182.7 2.4 collective-permute-start.4
  185.1 3.4 fusion.10
  188.5 1.4 slice_bitcast_fusion.36
  189.9 2.8 fusion.11
  192.7 1.4 slice_bitcast_fusion.39
  194.1 1.4 fusion.12
  195.5 1.4 slice_bitcast_fusion.42
  197.5 88.2 %all-gather.6.cloned.1.call-done = bf16[3,3,1024,256]{3,2,1,0:T(8,128)(2,1)} async-done(((bf16[3,3,32,256]{3,2,1,0:T(8,128)(2,1)}), bf16[3,3,1024,256]{3,2,1,0:T(8,128)(2,1)}) %all-gather.6.cloned.1.call-update) | async-done | bytes 4718608 | tf_op jit(solution)/shard_map/all_gather | solution.py:100
  285.6 3.4 fusion.7
  289.1 1.4 slice_bitcast_fusion.27
  290.5 2.8 fusion.8
  293.3 1.4 slice_bitcast_fusion.30
  294.7 1.4 fusion.9
  296.1 1.4 slice_bitcast_fusion.33
  298.1 63.8 %all-gather.8.cloned.1.call-done = bf16[3,3,1024,256]{3,2,1,0:T(8,128)(2,1)} async-done(((bf16[3,3,32,256]{3,2,1,0:T(8,128)(2,1)}), bf16[3,3,1024,256]{3,2,1,0:T(8,128)(2,1)}) %all-gather.8.cloned.1.call-update) | async-done | bytes 4718608 | tf_op jit(solution)/shard_map/all_gather | solution.py:101
  361.9 3.4 fusion.4
  365.5 2.8 fusion.5
  368.4 1.4 fusion.6
  371.7 2.3 fusion.26
  374.7 1.9 fusion.34
  382.0 237.9 %all-reduce.23.cloned.1.call-done = (f32[16,1024]{1,0:T(8,128)}, f32[16,1024]{1,0:T(8,128)}) async-done(((f32[16,1024]{1,0:T(8,128)}, f32[16,1024]{1,0:T(8,128)}), (f32[16,1024]{1,0:T(8,128)}, f32[16,1024]{1,0:T(8,128)})) %all-reduce.23.cloned.1.call-update) | async-done | bytes 131088 | tf_op jit(solution)/shard_map/psum | solution.py:118
  622.0 1.7 maximum_convert_fusion
  625.0 44.1 %all-reduce.20 = (f32[16,256]{1,0:T(8,128)S(1)}, f32[16,256]{1,0:T(8,128)S(1)}) all-reduce(f32[16,256]{1,0:T(8,128)S(1)} %fusion.76, f32[16,256]{1,0:T(8,128)S(1)} %fusion.77), channel_id=1, replica_groups=mesh['dp'=32,'rows'=8] {'rows'}, use_global_device_ids=true, to_apply=%region_10.11 | all-reduce | flops 8192 | bytes 65536 | tf_op jit(solution)/shard_map/psum | solution.py:66
  669.1 135.1 %all-reduce.19 = (f32[16,256]{1,0:T(8,128)S(1)}, f32[16,256]{1,0:T(8,128)S(1)}) all-reduce(f32[16,256]{1,0:T(8,128)S(1)} %get-tuple-element.13, f32[16,256]{1,0:T(8,128)S(1)} %get-tuple-element.14), channel_id=1, replica_groups=mesh['dp'=32,'rows'=8] {'dp'}, use_global_device_ids=true, to_apply=%region_11.12 | all-reduce | flops 8192 | bytes 65536 | tf_op jit(solution)/shard_map/psum | solution.py:65
  805.2 22.8 %all_to_all.18 = bf16[2,6,64,256]{3,0,1,2:T(2,128)(2,1)S(1)} all-to-all(bf16[2,6,64,256]{3,0,1,2:T(2,128)(2,1)S(1)} %copy.97), channel_id=1, replica_groups=mesh['dp'=32,'rows'=8] {'dp'}, dimensions={2} | all-to-all | bytes 786432 | tf_op jit(solution)/shard_map/all_to_all | solution.py:139
  (92 shorter events, 18.9 us)
Async XLA Ops:
  6.5 617.2 %copy-start = (bf16[1280,256]{1,0:T(8,128)(2,1)S(1)}, bf16[1280,256]{1,0:T(8,128)(2,1)}, u32[]{:S(2)}) copy-start(bf16[1280,256]{1,0:T(8,128)(2,1)} %param.18) | copy-start | bytes 1966084
  6.5 178.6 %all-gather.4.cloned.1.call-start = ((), (), s32[]{:S(2)}) async-start(), calls=%async_computation.1 | async-start | bytes 4866048 | tf_op jit(solution)/shard_map/all_gather | solution.py:99
  7.3 278.4 %all-gather.6.cloned.1.call-start = ((), (), s32[]{:S(2)}) async-start(), calls=%async_computation.2 | async-start | bytes 4866048 | tf_op jit(solution)/shard_map/all_gather | solution.py:100
  8.0 174.6 %copy-start.2 = (bf16[2,6,64,1024]{3,2,1,0:T(8,128)(2,1)S(1)}, bf16[2,6,64,1024]{3,2,1,0:T(8,128)(2,1)}, u32[]{:S(2)}) copy-start(bf16[2,6,64,1024]{3,2,1,0:T(8,128)(2,1)} %param.12) | copy-start | bytes 4718596
  8.0 353.8 %all-gather.8.cloned.1.call-start = ((), (), s32[]{:S(2)}) async-start(), calls=%async_computation.3 | async-start | bytes 4866048 | tf_op jit(solution)/shard_map/all_gather | solution.py:101
  8.8 611.1 %all-reduce.23.cloned.1.call-start = ((), (), s32[]{:S(2)}) async-start(), calls=%async_computation.4 | async-start | bytes 262144 | tf_op jit(solution)/shard_map/psum | solution.py:118
  8.8 173.8 %collective-permute-start.1 = (bf16[2,6,64,1024]{3,2,1,0:T(8,128)(2,1)}, bf16[2,6,64,1024]{3,2,1,0:T(8,128)(2,1)}, u32[]{:S(2)}, u32[]{:S(2)}) collective-permute-start(bf16[2,6,64,1024]{3,2,1,0:T(8,128)(2,1)} %param.12), channel_id=1, source_target_pairs={{2,0},{3,1},{4,2},{5,3},{6,4},{7,5},{10,8},{11,9},{12,10},{13,11},... | collective-permute-start | bytes 4718600 | tf_op jit(solution)/shard_map/ppermute | solution.py:14
  10.1 179.8 %collective-permute-start = (bf16[2,6,64,1024]{3,2,1,0:T(8,128)(2,1)}, bf16[2,6,64,1024]{3,2,1,0:T(8,128)(2,1)}, u32[]{:S(2)}, u32[]{:S(2)}) collective-permute-start(bf16[2,6,64,1024]{3,2,1,0:T(8,128)(2,1)} %param.12), channel_id=1, source_target_pairs={{0,2},{1,3},{2,4},{3,5},{4,6},{5,7},{8,10},{9,11},{10,12},{11,13},... | collective-permute-start | bytes 4718600 | tf_op jit(solution)/shard_map/ppermute | solution.py:14
  17.6 179.9 %collective-permute-start.3 = (bf16[2,6,64,1024]{3,2,1,0:T(8,128)(2,1)}, bf16[2,6,64,1024]{3,2,1,0:T(8,128)(2,1)}, u32[]{:S(2)}, u32[]{:S(2)}) collective-permute-start(bf16[2,6,64,1024]{3,2,1,0:T(8,128)(2,1)} %param.12), channel_id=1, source_target_pairs={{4,0},{5,1},{6,2},{7,3},{12,8},{13,9},{14,10},{15,11},{20,16},{21,... | collective-permute-start | bytes 4718600 | tf_op jit(solution)/shard_map/ppermute | solution.py:14
  18.9 271.6 %collective-permute-start.2 = (bf16[2,6,64,1024]{3,2,1,0:T(8,128)(2,1)}, bf16[2,6,64,1024]{3,2,1,0:T(8,128)(2,1)}, u32[]{:S(2)}, u32[]{:S(2)}) collective-permute-start(bf16[2,6,64,1024]{3,2,1,0:T(8,128)(2,1)} %param.12), channel_id=1, source_target_pairs={{0,4},{1,5},{2,6},{3,7},{8,12},{9,13},{10,14},{11,15},{16,20},{17,... | collective-permute-start | bytes 4718600 | tf_op jit(solution)/shard_map/ppermute | solution.py:14
  30.1 267.9 %collective-permute-start.5 = (bf16[2,6,64,1024]{3,2,1,0:T(8,128)(2,1)}, bf16[2,6,64,1024]{3,2,1,0:T(8,128)(2,1)}, u32[]{:S(2)}, u32[]{:S(2)}) collective-permute-start(bf16[2,6,64,1024]{3,2,1,0:T(8,128)(2,1)} %param.12), channel_id=1, source_target_pairs={{6,0},{7,1},{14,8},{15,9},{22,16},{23,17},{30,24},{31,25},{38,32},... | collective-permute-start | bytes 4718600 | tf_op jit(solution)/shard_map/ppermute | solution.py:14
  182.7 182.8 %collective-permute-start.4 = (bf16[2,6,64,1024]{3,2,1,0:T(8,128)(2,1)S(1)}, bf16[2,6,64,1024]{3,2,1,0:T(8,128)(2,1)}, u32[]{:S(2)}, u32[]{:S(2)}) collective-permute-start(bf16[2,6,64,1024]{3,2,1,0:T(8,128)(2,1)S(1)} %copy-done.2), channel_id=1, source_target_pairs={{0,6},{1,7},{8,14},{9,15},{16,22},{17,23},{24,30},{25,31},{32,38},... | collective-permute-start | bytes 4718600 | tf_op jit(solution)/shard_map/ppermute | solution.py:14
  185.1 4.8 copy-start.26
  188.5 4.2 copy-start.15
  192.7 2.8 copy-start.16
  195.5 2.0 copy-start.17
  285.6 4.9 copy-start.25
  289.1 4.2 copy-start.18
  293.3 2.8 copy-start.19
  296.1 1.9 copy-start.20
  361.9 3.6 copy-start.24
  368.4 1.6 copy-start.7
  369.9 1.8 copy-start.6
  371.7 2.3 copy-start.9
  371.7 2.3 copy-start.10
  371.7 2.3 copy-start.11
  371.7 2.5 copy-start.12
  371.7 2.8 copy-start.13
  371.7 3.0 copy-start.14
  378.1 2.2 copy-start.21
  623.8 180.8 %copy-start.22 = (f32[256]{0:T(256)S(1)}, f32[256]{0:T(256)}, u32[]{:S(2)}) copy-start(f32[256]{0:T(256)} %param.22) | copy-start | bytes 3076
  623.8 180.8 %copy-start.23 = (f32[256]{0:T(256)S(1)}, f32[256]{0:T(256)}, u32[]{:S(2)}) copy-start(f32[256]{0:T(256)} %param.21) | copy-start | bytes 3076
  (5 other events, 6.6 us)
Sparse Core Ops, SparseCore 0:
  9.2 141.1 all-gather.3
  152.3 133.2 all-gather.5
  287.5 74.2 all-gather.7
  380.5 239.3 all-reduce.22
